TPU v7x, 32 devices: a whole 2x2x4 slice. The times are simulated.
32 devices in a mesh: seq: 8 (over z, x), head: 4 (over y, core).
Axes of the slice: x: 2, y: 2, z: 4, core: 2. Of those that a mesh axis runs over, the one named last changes fastest.
Arguments:
- queries: bfloat16 [8192, 8192], P('seq', 'head'), may hold values from -0.5390625 to 0.5390625
- keys: bfloat16 [8192, 8192], P('seq', 'head'), may hold values from -0.5390625 to 0.5390625
- values: bfloat16 [8192, 8192], P('seq', 'head'), may hold values from -6 to 6
- log_decay: float32 [8192, 64], P('seq', 'head'), may hold values from -1 to 0
- gain: float32 [8192], P('head'), may hold values from 0.1 to 1.9
- lengths: int32 [8], replicated, may hold values from 1 to 2048, 8192 in all
- out_grad: bfloat16 [8192, 8192], P('seq', 'head'), may hold values from -6 to 6
Outputs:
- normed: bfloat16 [8192, 8192], P('seq', 'head')
- grad_query: bfloat16 [8192, 8192], P('seq', 'head')
- grad_key: bfloat16 [8192, 8192], P('seq', 'head')
- grad_value: bfloat16 [8192, 8192], P('seq', 'head')
Inputs may be any that keep to these rules, and one draw needn't show every extreme that they name: The 8 lengths sum to 8192.
All inputs are finite; a program needn't handle non-finite values.
Results may differ from a plain program's by a relative error of at most 0.012.
Values sent between devices are 32-bit elements; how exact they have to be, the bound alone decides.
No kernel may reach another device: no remote copies, remote signals or barrier semaphores. Data moves between devices by JAX's collectives and lax.ppermute only.
A program may use at most 192 MiB of HBM per device.

v0:
```python
import functools

import jax
import jax.numpy as jnp
from jax import lax
from jax.experimental import pallas as pl
from jax.experimental.pallas import tpu as pltpu
from jax.sharding import PartitionSpec as P

BLOCK = 128
LANES = 128
EPS = 1e-06
F32 = jnp.float32
BF16 = jnp.bfloat16
VMEM_LIMIT = 58 * 1024 * 1024
DOC_SHARE = 4


def dot_nn(left, right):
    return lax.dot_general(left, right, (((1,), (0,)), ((), ())), preferred_element_type=F32)


def dot_nt(left, right):
    return lax.dot_general(left, right, (((1,), (1,)), ((), ())), preferred_element_type=F32)


def dot_tn(left, right):
    return lax.dot_general(left, right, (((0,), (0,)), ((), ())), preferred_element_type=F32)


def head_cols(index, size):
    return slice(index * size, (index + 1) * size)


def scaled_half(array, factor):
    return (array.astype(F32) * factor).astype(BF16)


def spec(shape, index_map):
    return pl.BlockSpec(shape, index_map)


def whole_spec(shape):
    rank = len(shape)
    return pl.BlockSpec(shape, lambda i: (0,) * rank)


def params():
    return pltpu.CompilerParams(vmem_limit_bytes=VMEM_LIMIT)


def cost(flops, bytes_accessed):
    return pl.CostEstimate(flops=flops, bytes_accessed=bytes_accessed, transcendentals=0)


RUN, ENTER, LEAVE, ENTER_DEV, LEAVE_DEV = range(5)


def count_docs(place, ends):
    total = jnp.zeros_like(place)
    for end in ends:
        total = total + (place >= end).astype(jnp.int32)
    return total


def write_factors(heads, docs, rate_ref, len_ref, first_ref, col_ref, row_ref, keep_ref, keep_dev_ref):
    rows = rate_ref.shape[0]
    blocks = rows // BLOCK
    first = first_ref[0]
    ends, total = [], 0
    for i in range(docs):
        total = total + len_ref[i]
        ends.append(total)

    def doc_at(place):
        return jnp.where(place >= 0, count_docs(place, ends), -1)

    tri = (
        lax.broadcasted_iota(jnp.int32, (BLOCK, BLOCK), 0)
        >= lax.broadcasted_iota(jnp.int32, (BLOCK, BLOCK), 1)
    ).astype(F32)
    runs, offsets = [], []
    offset = jnp.zeros((1, heads), F32)
    for b in range(blocks):
        rates = rate_ref[b * BLOCK : (b + 1) * BLOCK, :]
        run = lax.dot_general(
            tri, rates, (((1,), (0,)), ((), ())),
            precision=lax.Precision.HIGHEST, preferred_element_type=F32,
        )
        run_rows = lax.dot_general(
            rates, tri, (((0,), (1,)), ((), ())),
            precision=lax.Precision.HIGHEST, preferred_element_type=F32,
        )
        row_ref[0:heads, b * BLOCK : (b + 1) * BLOCK] = run_rows
        runs.append(run)
        offsets.append(offset)
        offset = offset + run[BLOCK - 1 : BLOCK, :]
    doc_before = doc_at(first - 1)
    doc_end = doc_at(first + rows - 1)
    prefix = jnp.ones((1, heads), F32)
    keep_ref[...] = jnp.zeros_like(keep_ref)
    keep_dev = jnp.exp(offset) * (doc_end == doc_before).astype(F32)
    keep_dev_ref[...] = jnp.zeros_like(keep_dev_ref)
    keep_dev_ref[0:1, 0:heads] = keep_dev
    for b in range(blocks):
        low = b * BLOCK
        rows_at = slice(low, low + BLOCK)
        place = first + low + lax.broadcasted_iota(jnp.int32, (BLOCK, 1), 0)
        doc = count_docs(place, ends)
        doc_start = doc_at(first + low - 1)
        doc_last = doc_at(first + low + BLOCK - 1)
        run = runs[b]
        last = run[BLOCK - 1 : BLOCK, :]
        run_dev = offsets[b] + run
        groups = (
            run,
            jnp.exp(run) * (doc == doc_start).astype(F32),
            jnp.exp(last - run) * (doc == doc_last).astype(F32),
            jnp.exp(run_dev) * (doc == doc_before).astype(F32),
            jnp.exp(offset - run_dev) * (doc == doc_end).astype(F32),
        )
        for g, group in enumerate(groups):
            col_ref[rows_at, g * heads : (g + 1) * heads] = group
        col_ref[rows_at, len(groups) * heads : len(groups) * heads + 1] = doc.astype(F32)
        keep = jnp.exp(last) * (doc_last == doc_start).astype(F32)
        keep_ref[b, 0:1, 0:heads] = keep
        keep_ref[b, 1:2, 0:heads] = prefix
        prefix = prefix * keep
    place = first + lax.broadcasted_iota(jnp.int32, (1, rows), 1)
    row_ref[heads : heads + 1, :] = count_docs(place, ends).astype(F32)


def state_kernel(
    heads, size, docs, len_ref, first_ref, rate_ref, key_ref, value_ref,
    state_ref, col_ref, row_ref, keep_ref, keep_dev_ref,
):
    step = pl.program_id(0)
    rows = key_ref.shape[0]

    @pl.when(step == 0)
    def _():
        write_factors(heads, docs, rate_ref, len_ref, first_ref, col_ref, row_ref, keep_ref, keep_dev_ref)
        state_ref[...] = jnp.zeros_like(state_ref)

    col = col_ref[pl.ds(pl.multiple_of(step * rows, rows), rows), :]
    for h in range(heads):
        leave = col[:, LEAVE_DEV * heads + h : LEAVE_DEV * heads + h + 1]
        weighted = scaled_half(key_ref[:, head_cols(h, size)], leave)
        state_ref[h] += dot_tn(weighted, value_ref[:, head_cols(h, size)])


def local_states(keys, values, rates, lengths, first, heads, size):
    rows, width = keys.shape
    docs = lengths.shape[0]
    step_rows = min(256, rows)
    blocks = rows // BLOCK
    row_count = -(-(heads + 1) // 8) * 8
    shapes = (
        (heads, size, size),
        (rows, LANES),
        (row_count, rows),
        (blocks, 8, LANES),
        (8, LANES),
    )
    smem = pl.BlockSpec(memory_space=pltpu.SMEM)
    return pl.pallas_call(
        functools.partial(state_kernel, heads, size, docs),
        grid=(rows // step_rows,),
        in_specs=[
            smem,
            smem,
            whole_spec((rows, heads)),
            spec((step_rows, width), lambda i: (i, 0)),
            spec((step_rows, width), lambda i: (i, 0)),
        ],
        out_specs=[whole_spec(s) for s in shapes],
        out_shape=[jax.ShapeDtypeStruct(s, F32) for s in shapes],
        compiler_params=params(),
        cost_estimate=cost(2 * rows * width * size, 4 * rows * width),
        name="local_state",
    )(lengths, first, rates, keys, values)


def block_weights(heads, col, rows_ref, h, bias):
    return jnp.exp(col[:, RUN * heads + h : RUN * heads + h + 1] - rows_ref[h : h + 1, :] + bias)


def block_bias(heads, col, rows_ref):
    doc_col = col[:, 5 * heads : 5 * heads + 1]
    doc_row = rows_ref[heads : heads + 1, :]
    causal = lax.broadcasted_iota(jnp.int32, (BLOCK, BLOCK), 0) >= lax.broadcasted_iota(
        jnp.int32, (BLOCK, BLOCK), 1
    )
    return jnp.where(causal & (doc_col == doc_row), 0.0, -1e30)


def forward_kernel(
    heads, size, query_ref, key_ref, value_ref, col_ref, row_ref, keep_ref,
    raw_ref, probs_ref, states_ref, state_ref,
):
    step = pl.program_id(0)

    @pl.when(step == 0)
    def _():
        state_ref[...] = jnp.zeros_like(state_ref)

    col = col_ref[...]
    bias = block_bias(heads, col, row_ref)
    for h in range(heads):
        at = head_cols(h, size)
        query, key, value = query_ref[:, at], key_ref[:, at], value_ref[:, at]
        enter = col[:, ENTER * heads + h : ENTER * heads + h + 1]
        leave = col[:, LEAVE * heads + h : LEAVE * heads + h + 1]
        weights = block_weights(heads, col, row_ref, h, bias)
        probs = (dot_nt(query, key) * weights).astype(BF16)
        state = state_ref[h]
        state_half = state.astype(BF16)
        probs_ref[0, h] = probs
        states_ref[0, h] = state_half
        both = jnp.concatenate([probs, scaled_half(query, enter)], axis=1)
        raw = dot_nn(both, jnp.concatenate([value, state_half], axis=0))
        raw_ref[:, at] = raw.astype(BF16)
        state_ref[h] = keep_ref[0, 0:1, h : h + 1] * state + dot_tn(scaled_half(key, leave), value)


def forward_local(queries, keys, values, col, row, keep, heads, size):
    rows, width = queries.shape
    blocks = rows // BLOCK
    token = spec((BLOCK, width), lambda i: (i, 0))
    per_block = spec((1, heads, size, size), lambda i: (i, 0, 0, 0))
    return pl.pallas_call(
        functools.partial(forward_kernel, heads, size),
        grid=(blocks,),
        in_specs=[
            token,
            token,
            token,
            spec((BLOCK, LANES), lambda i: (i, 0)),
            spec((row.shape[0], BLOCK), lambda i: (0, i)),
            spec((1, 8, LANES), lambda i: (i, 0, 0)),
        ],
        out_specs=[token, per_block, per_block],
        out_shape=[
            jax.ShapeDtypeStruct((rows, width), BF16),
            jax.ShapeDtypeStruct((blocks, heads, BLOCK, BLOCK), BF16),
            jax.ShapeDtypeStruct((blocks, heads, size, size), BF16),
        ],
        scratch_shapes=[pltpu.VMEM((heads, size, size), F32)],
        compiler_params=params(),
        cost_estimate=cost(8 * rows * width * size, 12 * rows * width),
        name="forward_local",
    )(queries, keys, values, col, row, keep)


def horner(received, keeps, h):
    total = received[-1][h]
    for state, keep in zip(reversed(received[:-1]), reversed(keeps)):
        total = state[h] + keep[0:1, h : h + 1] * total
    return total


def raw_kernel(heads, size, hops, raw_ref, query_ref, grad_ref, gain_ref, col_ref, *rest):
    received, keeps = rest[:hops], rest[hops : 2 * hops - 1]
    out_ref, sums_ref, enter_ref = rest[2 * hops - 1 :]
    step = pl.program_id(0)
    rows = raw_ref.shape[0]

    @pl.when(step == 0)
    def _():
        for h in range(heads):
            enter_ref[h] = horner(received, keeps, h).astype(BF16)

    col = col_ref[...]
    squares = jnp.zeros((rows, size), F32)
    projected = jnp.zeros((rows, size), F32)
    for h in range(heads):
        at = head_cols(h, size)
        enter = col[:, ENTER_DEV * heads + h : ENTER_DEV * heads + h + 1]
        raw = raw_ref[:, at].astype(F32) + enter * dot_nn(query_ref[:, at], enter_ref[h])
        out_ref[:, at] = raw.astype(BF16)
        squares = squares + raw * raw
        projected = projected + grad_ref[:, at].astype(F32) * gain_ref[:, at] * raw
    lane = lax.broadcasted_iota(jnp.int32, (rows, LANES), 1)
    packed = jnp.where(
        lane == 0,
        jnp.sum(squares, axis=1, keepdims=True),
        jnp.where(lane == 1, jnp.sum(projected, axis=1, keepdims=True), 0.0),
    )
    sums_ref[...] = packed.T[0:8, :]


def raw_and_sums(raw, queries, out_grad, gain, col, received, keeps, heads, size):
    rows, width = queries.shape
    step_rows = min(256, rows)
    token = spec((step_rows, width), lambda i: (i, 0))
    state_shape = (heads, size, size)
    return pl.pallas_call(
        functools.partial(raw_kernel, heads, size, len(received)),
        grid=(rows // step_rows,),
        in_specs=[
            token,
            token,
            token,
            whole_spec((1, width)),
            spec((step_rows, LANES), lambda i: (i, 0)),
        ]
        + [whole_spec(state_shape)] * len(received)
        + [whole_spec((8, LANES))] * len(keeps),
        out_specs=[token, spec((8, step_rows), lambda i: (0, i)), whole_spec(state_shape)],
        out_shape=[
            jax.ShapeDtypeStruct((rows, width), BF16),
            jax.ShapeDtypeStruct((8, rows), F32),
            jax.ShapeDtypeStruct(state_shape, BF16),
        ],
        compiler_params=params(),
        cost_estimate=cost(2 * rows * width * size, 8 * rows * width),
        name="raw_and_sums",
    )(raw, queries, out_grad, gain, col, *received, *keeps)


def carry_kernel(heads, size, full_width, parts, raw_ref, query_ref, grad_ref, gain_ref, col_ref, *rest):
    sums = rest[:parts]
    carry_ref, scale_ref = rest[parts:]
    step = pl.program_id(0)
    rows = raw_ref.shape[0]

    @pl.when(step == 0)
    def _():
        carry_ref[...] = jnp.zeros_like(carry_ref)

    total = sums[0][...]
    for part in sums[1:]:
        total = total + part[...]
    total = jnp.concatenate([total, jnp.zeros((LANES - 8, rows), F32)], axis=0).T
    inverse = lax.rsqrt(total[:, 0:1] / full_width + EPS)
    slope = inverse * inverse * inverse * total[:, 1:2] / full_width
    lane = lax.broadcasted_iota(jnp.int32, (rows, LANES), 1)
    scale_ref[...] = jnp.where(lane == 0, inverse, slope)
    col = col_ref[...]
    for h in range(heads):
        at = head_cols(h, size)
        enter = col[:, ENTER_DEV * heads + h : ENTER_DEV * heads + h + 1]
        scaled = grad_ref[:, at].astype(F32) * gain_ref[:, at]
        grad_raw = (inverse * scaled - raw_ref[:, at].astype(F32) * slope).astype(BF16)
        carry_ref[h] += dot_tn(scaled_half(query_ref[:, at], enter), grad_raw)


def carry_states(raw, queries, out_grad, gain, col, sums, full_width, heads, size):
    rows, width = queries.shape
    step_rows = min(256, rows)
    token = spec((step_rows, width), lambda i: (i, 0))
    narrow = spec((step_rows, LANES), lambda i: (i, 0))
    state_shape = (heads, size, size)
    return pl.pallas_call(
        functools.partial(carry_kernel, heads, size, full_width, len(sums)),
        grid=(rows // step_rows,),
        in_specs=[token, token, token, whole_spec((1, width)), narrow]
        + [spec((8, step_rows), lambda i: (0, i))] * len(sums),
        out_specs=[whole_spec(state_shape), narrow],
        out_shape=[
            jax.ShapeDtypeStruct(state_shape, F32),
            jax.ShapeDtypeStruct((rows, LANES), F32),
        ],
        compiler_params=params(),
        cost_estimate=cost(2 * rows * width * size, 6 * rows * width),
        name="carry_state",
    )(raw, queries, out_grad, gain, col, *sums)


def backward_kernel(
    heads, size, query_ref, key_ref, value_ref, raw_ref, out_grad_ref, gain_ref, scale_ref,
    col_ref, row_ref, keep_ref, probs_ref, states_ref, enter_ref,
    normed_ref, grad_query_ref, grad_key_ref, grad_value_ref, carry_ref,
):
    step = pl.program_id(0)

    @pl.when(step == 0)
    def _():
        carry_ref[...] = jnp.zeros_like(carry_ref)

    col = col_ref[...]
    bias = block_bias(heads, col, row_ref)
    inverse, slope = scale_ref[:, 0:1], scale_ref[:, 1:2]
    for h in range(heads):
        at = head_cols(h, size)
        query, key, value = query_ref[:, at], key_ref[:, at], value_ref[:, at]
        raw, gain = raw_ref[:, at].astype(F32), gain_ref[:, at]
        enter = col[:, ENTER * heads + h : ENTER * heads + h + 1]
        leave = col[:, LEAVE * heads + h : LEAVE * heads + h + 1]
        grad_raw = (inverse * (out_grad_ref[:, at].astype(F32) * gain) - raw * slope).astype(BF16)
        normed_ref[:, at] = (raw * inverse * gain).astype(BF16)
        weights = block_weights(heads, col, row_ref, h, bias)
        mixed = (dot_nt(grad_raw, value) * weights).astype(BF16)
        prefix = keep_ref[0, 1:2, h : h + 1]
        state = (states_ref[0, h].astype(F32) + prefix * enter_ref[h].astype(F32)).astype(BF16)
        grad_query = dot_nn(mixed, key) + enter * dot_nt(grad_raw, state)
        grad_query_ref[:, at] = grad_query.astype(BF16)
        carry = carry_ref[h]
        carry_half = carry.astype(BF16)
        grad_key = dot_tn(mixed, query) + leave * dot_nt(value, carry_half)
        grad_value = dot_tn(probs_ref[0, h], grad_raw) + leave * dot_nn(key, carry_half)
        grad_key_ref[:, at] = grad_key.astype(BF16)
        grad_value_ref[:, at] = grad_value.astype(BF16)
        carry_ref[h] = keep_ref[0, 0:1, h : h + 1] * carry + dot_tn(scaled_half(query, enter), grad_raw)


def backward_local(
    queries, keys, values, raw, out_grad, gain, scale, col, row, keep, probs, states, entering, heads, size
):
    rows, width = queries.shape
    blocks = rows // BLOCK
    token = spec((BLOCK, width), lambda i: (blocks - 1 - i, 0))
    narrow = spec((BLOCK, LANES), lambda i: (blocks - 1 - i, 0))
    per_block = spec((1, heads, size, size), lambda i: (blocks - 1 - i, 0, 0, 0))
    return pl.pallas_call(
        functools.partial(backward_kernel, heads, size),
        grid=(blocks,),
        in_specs=[
            token,
            token,
            token,
            token,
            token,
            whole_spec((1, width)),
            narrow,
            narrow,
            spec((row.shape[0], BLOCK), lambda i: (0, blocks - 1 - i)),
            spec((1, 8, LANES), lambda i: (blocks - 1 - i, 0, 0)),
            per_block,
            per_block,
            whole_spec((heads, size, size)),
        ],
        out_specs=[token] * 4,
        out_shape=[jax.ShapeDtypeStruct((rows, width), BF16)] * 4,
        scratch_shapes=[pltpu.VMEM((heads, size, size), F32)],
        compiler_params=params(),
        cost_estimate=cost(16 * rows * width * size, 22 * rows * width),
        name="backward_local",
    )(queries, keys, values, raw, out_grad, gain, scale, col, row, keep, probs, states, entering)


def finish_kernel(heads, size, hops, key_ref, value_ref, grad_key_ref, grad_value_ref, col_ref, *rest):
    received, keeps = rest[:hops], rest[hops : 2 * hops - 1]
    key_out_ref, value_out_ref, beyond_ref = rest[2 * hops - 1 :]
    step = pl.program_id(0)

    @pl.when(step == 0)
    def _():
        for h in range(heads):
            beyond_ref[h] = horner(received, keeps, h).astype(BF16)

    col = col_ref[...]
    for h in range(heads):
        at = head_cols(h, size)
        leave = col[:, LEAVE_DEV * heads + h : LEAVE_DEV * heads + h + 1]
        beyond = beyond_ref[h]
        grad_key = grad_key_ref[:, at].astype(F32) + leave * dot_nt(value_ref[:, at], beyond)
        grad_value = grad_value_ref[:, at].astype(F32) + leave * dot_nn(key_ref[:, at], beyond)
        key_out_ref[:, at] = grad_key.astype(BF16)
        value_out_ref[:, at] = grad_value.astype(BF16)


def finish(keys, values, grad_key, grad_value, col, received, keeps, heads, size):
    rows, width = keys.shape
    step_rows = min(256, rows)
    token = spec((step_rows, width), lambda i: (i, 0))
    state_shape = (heads, size, size)
    return pl.pallas_call(
        functools.partial(finish_kernel, heads, size, len(received)),
        grid=(rows // step_rows,),
        in_specs=[token] * 4
        + [spec((step_rows, LANES), lambda i: (i, 0))]
        + [whole_spec(state_shape)] * len(received)
        + [whole_spec((8, LANES))] * len(keeps),
        out_specs=[token, token],
        out_shape=[jax.ShapeDtypeStruct((rows, width), BF16)] * 2,
        scratch_shapes=[pltpu.VMEM(state_shape, BF16)],
        compiler_params=params(),
        cost_estimate=cost(4 * rows * width * size, 12 * rows * width),
        name="finish",
    )(keys, values, grad_key, grad_value, col, *received, *keeps)


def from_shards(value, count, away):
    pairs = [(i, i + away) for i in range(count) if 0 <= i + away < count]
    return lax.ppermute(value, "seq", pairs)


def body(queries, keys, values, log_decay, gain, lengths, out_grad):
    rows, heads = log_decay.shape
    width = queries.shape[1]
    size = width // heads
    count = lax.axis_size("seq")
    groups = lax.axis_size("head")
    full_width = width * groups
    longest = rows * count // DOC_SHARE
    hops = max(1, min(count - 1, -(-(longest - 1) // rows)))
    first = (lax.axis_index("seq") * rows).astype(jnp.int32).reshape(1)
    gain = gain.reshape(1, width)

    state, col, row, keep, keep_dev = local_states(keys, values, log_decay, lengths, first, heads, size)
    before = [from_shards(state, count, j) for j in range(1, hops + 1)]
    keep_before = [from_shards(keep_dev, count, j) for j in range(1, hops)]
    keep_after = [from_shards(keep_dev, count, -j) for j in range(1, hops)]
    raw, probs, states = forward_local(queries, keys, values, col, row, keep, heads, size)
    raw, sums, entering = raw_and_sums(raw, queries, out_grad, gain, col, before, keep_before, heads, size)
    every = [sums] + [
        lax.ppermute(sums, "head", [(i, (i + j) % groups) for i in range(groups)]) for j in range(1, groups)
    ]
    carry, scale = carry_states(raw, queries, out_grad, gain, col, every, full_width, heads, size)
    after = [from_shards(carry, count, -j) for j in range(1, hops + 1)]
    normed, grad_query, grad_key, grad_value = backward_local(
        queries, keys, values, raw, out_grad, gain, scale, col, row, keep, probs, states, entering, heads, size
    )
    grad_key, grad_value = finish(keys, values, grad_key, grad_value, col, after, keep_after, heads, size)
    return (normed, grad_query, grad_key, grad_value)


def solution(mesh):
    token = P("seq", "head")
    in_specs = (token, token, token, token, P("head"), P(), token)
    return jax.shard_map(body, mesh=mesh, in_specs=in_specs, out_specs=(token,) * 4, check_vma=False)
```

profile of v0, /device:TPU:10, one launch (start us, length us, event | category | flops | bytes accessed | tf_op | source)
XLA Modules:
  0.0 157.3 jit_solution(17810146432375618548)
XLA Ops:
  0.6 1.8 %copy.11.rate_ref = f32[1024,16]{1,0:T(8,128)} copy(f32[1024,16]{0,1:T(8,128)} %param.10) | data formatting | bytes 131072 | tf_op args[3]
  2.5 11.6 %local_state.1 = (f32[16,128,128]{2,1,0:T(8,128)}, f32[1024,128]{1,0:T(8,128)}, f32[24,1024]{1,0:T(8,128)}, f32[8,8,128]{2,1,0:T(8,128)}, f32[8,128]{1,0:T(8,128)}) custom-call(s32[8]{0:T(128)} %len_ref.1, s32[1]{0:T(128)} %bitcast.first_ref, f32[1024,16]{1,0:T(8,128)} %copy.11.rate_ref, bf16[1024,2048]{1,0:T(8,128)(2,1)} %key_ref.7, ...), custom_call_target="tpu_custom_call" | custom-call | flops 536870912 | bytes 8388608 | tf_op jit(solution)/shard_map/local_state/pallas_call | solution.py:166
  14.1 3.5 %collective-permute-start = (f32[16,128,128]{2,1,0:T(8,128)}, f32[16,128,128]{2,1,0:T(8,128)S(1)}, u32[]{:S(2)}, u32[]{:S(2)}) collective-permute-start(f32[16,128,128]{2,1,0:T(8,128)} %get-tuple-element.27), channel_id=1, source_target_pairs={{0,4},{4,8},{8,12},{12,16},{16,20},{20,24},{24,28},{1,5},{5,9},{9,... | collective-permute-start | bytes 3145736 | tf_op jit(solution)/shard_map/ppermute | solution.py:486
  17.5 3.5 %collective-permute-start.1 = (f32[16,128,128]{2,1,0:T(8,128)}, f32[16,128,128]{2,1,0:T(8,128)S(1)}, u32[]{:S(2)}, u32[]{:S(2)}) collective-permute-start(f32[16,128,128]{2,1,0:T(8,128)} %get-tuple-element.27), channel_id=1, source_target_pairs={{0,8},{4,12},{8,16},{12,20},{16,24},{20,28},{1,9},{5,13},{9,17},{1... | collective-permute-start | bytes 3145736 | tf_op jit(solution)/shard_map/ppermute | solution.py:486
  21.0 3.4 %collective-permute-start.2 = (f32[8,128]{1,0:T(8,128)}, f32[8,128]{1,0:T(8,128)S(1)}, u32[]{:S(2)}, u32[]{:S(2)}) collective-permute-start(f32[8,128]{1,0:T(8,128)} %get-tuple-element.28), channel_id=1, source_target_pairs={{0,4},{4,8},{8,12},{12,16},{16,20},{20,24},{24,28},{1,5},{5,9},{9,... | collective-permute-start | bytes 12296 | tf_op jit(solution)/shard_map/ppermute | solution.py:486
  24.4 24.2 %forward_local.1 = (bf16[1024,2048]{1,0:T(8,128)(2,1)}, bf16[8,16,128,128]{3,2,1,0:T(8,128)(2,1)}, bf16[8,16,128,128]{3,2,1,0:T(8,128)(2,1)}) custom-call(bf16[1024,2048]{1,0:T(8,128)(2,1)} %query_ref.7, bf16[1024,2048]{1,0:T(8,128)(2,1)} %key_ref.7, bf16[1024,2048]{1,0:T(8,128)(2,1)} %value_ref.7, f32[1024,128]{1,0:T(8,128)} %get-tuple-element.23.col_ref, ...), custom_call_target="tpu_custom_call" | custom-call | flops 2147483648 | bytes 25165824 | tf_op jit(solution)/shard_map/forward_local/pallas_call | solution.py:231
  48.6 14.2 %collective-permute-done.2.rest_2_ = f32[8,128]{1,0:T(8,128)S(1)} collective-permute-done((f32[8,128]{1,0:T(8,128)}, f32[8,128]{1,0:T(8,128)S(1)}, u32[]{:S(2)}, u32[]{:S(2)}) %collective-permute-start.2) | collective-permute-done | bytes 4128 | tf_op jit(solution)/shard_map/ppermute | solution.py:486
  62.8 0.8 collective-permute-done.1.rest_1_
  63.7 0.8 copy-done.3
  64.5 10.2 %raw_and_sums.1 = (bf16[1024,2048]{1,0:T(8,128)(2,1)}, f32[8,1024]{1,0:T(8,128)}, bf16[16,128,128]{2,1,0:T(8,128)(2,1)}) custom-call(bf16[1024,2048]{1,0:T(8,128)(2,1)} %get-tuple-element.26.raw_ref, bf16[1024,2048]{1,0:T(8,128)(2,1)} %query_ref.7, bf16[1024,2048]{1,0:T(8,128)(2,1)} %out_grad_ref.1, f32[1,2048]{1,0:T(1,128)} %bitcast.2, ...), custom_call_target="tpu_custom_call" | custom-call | flops 536870912 | bytes 16777216 | tf_op jit(solution)/shard_map/raw_and_sums/pallas_call | solution.py:297
  74.8 1.6 %collective-permute-start.4 = (f32[8,1024]{1,0:T(8,128)}, f32[8,1024]{1,0:T(8,128)S(1)}, u32[]{:S(2)}, u32[]{:S(2)}) collective-permute-start(f32[8,1024]{1,0:T(8,128)} %get-tuple-element.30.rest_0_), channel_id=1, source_target_pairs={{0,2},{1,3},{2,0},{3,1},{4,6},{5,7},{6,4},{7,5},{8,10},{9,11},{10,... | collective-permute-start | bytes 98312 | tf_op jit(solution)/shard_map/ppermute | solution.py:508
  76.4 1.4 collective-permute-start.5
  77.8 0.6 collective-permute-done.3.rest_1_
  78.3 0.7 collective-permute-done.4.rest_2_
  79.0 0.7 collective-permute-done.5.rest_3_
  79.7 0.6 copy-done.6
  80.3 12.3 %carry_state.1 = (f32[16,128,128]{2,1,0:T(8,128)}, f32[1024,128]{1,0:T(8,128)}) custom-call(bf16[1024,2048]{1,0:T(8,128)(2,1)} %get-tuple-element.29.raw_ref, bf16[1024,2048]{1,0:T(8,128)(2,1)} %query_ref.7, bf16[1024,2048]{1,0:T(8,128)(2,1)} %out_grad_ref.1, f32[1,2048]{1,0:T(1,128)} %bitcast.3, f32[1024,128]{1,0:T(8,128)} %get-tuple-element.23.col_ref, ...), custom_call_target="tpu_custom_call" | custom-call | flops 536870912 | bytes 12582912 | tf_op jit(solution)/shard_map/carry_state/pallas_call | solution.py:354
  92.6 3.8 %collective-permute-start.6 = (f32[16,128,128]{2,1,0:T(8,128)}, f32[16,128,128]{2,1,0:T(8,128)S(1)}, u32[]{:S(2)}, u32[]{:S(2)}) collective-permute-start(f32[16,128,128]{2,1,0:T(8,128)} %get-tuple-element.39), channel_id=1, source_target_pairs={{4,0},{8,4},{12,8},{16,12},{20,16},{24,20},{28,24},{5,1},{9,5},{13... | collective-permute-start | bytes 3145736 | tf_op jit(solution)/shard_map/ppermute | solution.py:486
  96.3 1.9 %collective-permute-start.7 = (f32[16,128,128]{2,1,0:T(8,128)}, f32[16,128,128]{2,1,0:T(8,128)S(1)}, u32[]{:S(2)}, u32[]{:S(2)}) collective-permute-start(f32[16,128,128]{2,1,0:T(8,128)} %get-tuple-element.39), channel_id=1, source_target_pairs={{8,0},{12,4},{16,8},{20,12},{24,16},{28,20},{9,1},{13,5},{17,9},{2... | collective-permute-start | bytes 3145736 | tf_op jit(solution)/shard_map/ppermute | solution.py:486
  98.3 2.1 %collective-permute-start.8 = (f32[8,128]{1,0:T(8,128)S(1)}, f32[8,128]{1,0:T(8,128)S(1)}, u32[]{:S(2)}, u32[]{:S(2)}) collective-permute-start(f32[8,128]{1,0:T(8,128)S(1)} %copy-done.9), channel_id=1, source_target_pairs={{4,0},{8,4},{12,8},{16,12},{20,16},{24,20},{28,24},{5,1},{9,5},{13... | collective-permute-start | bytes 12296 | tf_op jit(solution)/shard_map/ppermute | solution.py:486
  100.4 30.5 %backward_local.1 = (bf16[1024,2048]{1,0:T(8,128)(2,1)}, bf16[1024,2048]{1,0:T(8,128)(2,1)}, bf16[1024,2048]{1,0:T(8,128)(2,1)}, bf16[1024,2048]{1,0:T(8,128)(2,1)}) custom-call(bf16[1024,2048]{1,0:T(8,128)(2,1)} %query_ref.7, bf16[1024,2048]{1,0:T(8,128)(2,1)} %key_ref.7, bf16[1024,2048]{1,0:T(8,128)(2,1)} %value_ref.7, ...), custom_call_target="tpu_custom_call" | custom-call | flops 4294967296 | bytes 46137344 | tf_op jit(solution)/shard_map/backward_local/pallas_call | solution.py:415
  130.9 13.0 %collective-permute-done.8.rest_2_ = f32[8,128]{1,0:T(8,128)S(1)} collective-permute-done((f32[8,128]{1,0:T(8,128)S(1)}, f32[8,128]{1,0:T(8,128)S(1)}, u32[]{:S(2)}, u32[]{:S(2)}) %collective-permute-start.8) | collective-permute-done | bytes 4128 | tf_op jit(solution)/shard_map/ppermute | solution.py:486
  144.0 0.6 copy-done.7
  145.3 12.0 %finish.1 = (bf16[1024,2048]{1,0:T(8,128)(2,1)}, bf16[1024,2048]{1,0:T(8,128)(2,1)}) custom-call(bf16[1024,2048]{1,0:T(8,128)(2,1)} %key_ref.7, bf16[1024,2048]{1,0:T(8,128)(2,1)} %value_ref.7, bf16[1024,2048]{1,0:T(8,128)(2,1)} %get-tuple-element.37.grad_key_ref, bf16[1024,2048]{1,0:T(8,128)(2,1)} %get-tuple-element.38.grad_value_ref, ...), custom_call_target="tpu_custom_call" | custom-call | flops 1073741824 | bytes 25165824 | tf_op jit(solution)/shard_map/finish/pallas_call | solution.py:468
  (21 shorter events, 1.0 us)
Async XLA Ops:
  14.1 48.7 %collective-permute-start = (f32[16,128,128]{2,1,0:T(8,128)}, f32[16,128,128]{2,1,0:T(8,128)S(1)}, u32[]{:S(2)}, u32[]{:S(2)}) collective-permute-start(f32[16,128,128]{2,1,0:T(8,128)} %get-tuple-element.27), channel_id=1, source_target_pairs={{0,4},{4,8},{8,12},{12,16},{16,20},{20,24},{24,28},{1,5},{5,9},{9,... | collective-permute-start | bytes 3145736 | tf_op jit(solution)/shard_map/ppermute | solution.py:486
  17.5 46.0 %collective-permute-start.1 = (f32[16,128,128]{2,1,0:T(8,128)}, f32[16,128,128]{2,1,0:T(8,128)S(1)}, u32[]{:S(2)}, u32[]{:S(2)}) collective-permute-start(f32[16,128,128]{2,1,0:T(8,128)} %get-tuple-element.27), channel_id=1, source_target_pairs={{0,8},{4,12},{8,16},{12,20},{16,24},{20,28},{1,9},{5,13},{9,17},{1... | collective-permute-start | bytes 3145736 | tf_op jit(solution)/shard_map/ppermute | solution.py:486
  21.0 41.7 %collective-permute-start.2 = (f32[8,128]{1,0:T(8,128)}, f32[8,128]{1,0:T(8,128)S(1)}, u32[]{:S(2)}, u32[]{:S(2)}) collective-permute-start(f32[8,128]{1,0:T(8,128)} %get-tuple-element.28), channel_id=1, source_target_pairs={{0,4},{4,8},{8,12},{12,16},{16,20},{20,24},{24,28},{1,5},{5,9},{9,... | collective-permute-start | bytes 12296 | tf_op jit(solution)/shard_map/ppermute | solution.py:486
  62.8 0.8 copy-start.8
  62.8 1.0 copy-start.2
  63.6 1.0 copy-start.3
  74.7 3.6 %collective-permute-start.3 = (f32[8,1024]{1,0:T(8,128)}, f32[8,1024]{1,0:T(8,128)S(1)}, u32[]{:S(2)}, u32[]{:S(2)}) collective-permute-start(f32[8,1024]{1,0:T(8,128)} %get-tuple-element.30.rest_0_), channel_id=1, source_target_pairs={{0,1},{1,2},{2,3},{3,0},{4,5},{5,6},{6,7},{7,4},{8,9},{9,10},{10,1... | collective-permute-start | bytes 98312 | tf_op jit(solution)/shard_map/ppermute | solution.py:508
  74.8 4.2 %collective-permute-start.4 = (f32[8,1024]{1,0:T(8,128)}, f32[8,1024]{1,0:T(8,128)S(1)}, u32[]{:S(2)}, u32[]{:S(2)}) collective-permute-start(f32[8,1024]{1,0:T(8,128)} %get-tuple-element.30.rest_0_), channel_id=1, source_target_pairs={{0,2},{1,3},{2,0},{3,1},{4,6},{5,7},{6,4},{7,5},{8,10},{9,11},{10,... | collective-permute-start | bytes 98312 | tf_op jit(solution)/shard_map/ppermute | solution.py:508
  76.4 3.3 %collective-permute-start.5 = (f32[8,1024]{1,0:T(8,128)}, f32[8,1024]{1,0:T(8,128)S(1)}, u32[]{:S(2)}, u32[]{:S(2)}) collective-permute-start(f32[8,1024]{1,0:T(8,128)} %get-tuple-element.30.rest_0_), channel_id=1, source_target_pairs={{0,3},{1,0},{2,1},{3,2},{4,7},{5,4},{6,5},{7,6},{8,11},{9,8},{10,9... | collective-permute-start | bytes 98312 | tf_op jit(solution)/shard_map/ppermute | solution.py:508
  78.3 1.4 copy-start.4
  79.0 0.7 copy-start.5
  79.7 0.6 copy-start.6
  80.3 18.0 %copy-start.9 = (f32[8,128]{1,0:T(8,128)S(1)}, f32[8,128]{1,0:T(8,128)}, u32[]{:S(2)}) copy-start(f32[8,128]{1,0:T(8,128)} %get-tuple-element.28) | copy-start | bytes 12292
  92.6 51.4 %collective-permute-start.6 = (f32[16,128,128]{2,1,0:T(8,128)}, f32[16,128,128]{2,1,0:T(8,128)S(1)}, u32[]{:S(2)}, u32[]{:S(2)}) collective-permute-start(f32[16,128,128]{2,1,0:T(8,128)} %get-tuple-element.39), channel_id=1, source_target_pairs={{4,0},{8,4},{12,8},{16,12},{20,16},{24,20},{28,24},{5,1},{9,5},{13... | collective-permute-start | bytes 3145736 | tf_op jit(solution)/shard_map/ppermute | solution.py:486
  96.3 47.6 %collective-permute-start.7 = (f32[16,128,128]{2,1,0:T(8,128)}, f32[16,128,128]{2,1,0:T(8,128)S(1)}, u32[]{:S(2)}, u32[]{:S(2)}) collective-permute-start(f32[16,128,128]{2,1,0:T(8,128)} %get-tuple-element.39), channel_id=1, source_target_pairs={{8,0},{12,4},{16,8},{20,12},{24,16},{28,20},{9,1},{13,5},{17,9},{2... | collective-permute-start | bytes 3145736 | tf_op jit(solution)/shard_map/ppermute | solution.py:486
  98.3 45.7 %collective-permute-start.8 = (f32[8,128]{1,0:T(8,128)S(1)}, f32[8,128]{1,0:T(8,128)S(1)}, u32[]{:S(2)}, u32[]{:S(2)}) collective-permute-start(f32[8,128]{1,0:T(8,128)S(1)} %copy-done.9), channel_id=1, source_target_pairs={{4,0},{8,4},{12,8},{16,12},{20,16},{24,20},{28,24},{5,1},{9,5},{13... | collective-permute-start | bytes 12296 | tf_op jit(solution)/shard_map/ppermute | solution.py:486
  143.9 0.6 copy-start.7
  143.9 1.0 copy-start
  144.0 1.3 copy-start.1
where the time goes:
time: 159 us; the launch traced here: 157 us
  Pallas kernels  101 us (64%)
  waiting for transfers between devices  29.9 us (19%)
  starting transfers between devices  21.1 us (13%)
  local copies, waits for them, and re-layouts  4.75 us (3%)
    pallas_call x1, Pallas kernels, backward_local(): pl.pallas_call(functools.partial(backward_kernel, heads, size), grid=(blo...  30.5 us
    ppermute x6, waiting for transfers between devices, from_shards(): return lax.ppermute(value, 'seq', pairs)  28 us
    pallas_call x1, Pallas kernels, forward_local(): pl.pallas_call(functools.partial(forward_kernel, heads, size), grid=(bloc...  24.2 us
    ppermute x6, starting transfers between devices, from_shards(): return lax.ppermute(value, 'seq', pairs)  18.1 us
    pallas_call x1, Pallas kernels, carry_states(): pl.pallas_call(functools.partial(carry_kernel, heads, size, full_width, l...  12.3 us
    pallas_call x1, Pallas kernels, finish(): pl.pallas_call(functools.partial(finish_kernel, heads, size, len(received...  12 us
    pallas_call x1, Pallas kernels, local_states(): pl.pallas_call(functools.partial(state_kernel, heads, size, docs), grid=(...  11.6 us
    pallas_call x1, Pallas kernels, raw_and_sums(): pl.pallas_call(functools.partial(raw_kernel, heads, size, len(received)),...  10.2 us
  transfers between devices with their start and end apart: 9, of which 6 were waited for; matrix products, arithmetic and copies ran while one was open for 0% of the time, Pallas kernels for 35%

commit v1 on v0

v1 whole, which is shorter than its diff:
```python
import functools

import jax
import jax.numpy as jnp
from jax import lax
from jax.experimental import pallas as pl
from jax.experimental.pallas import tpu as pltpu
from jax.sharding import PartitionSpec as P

BLOCK = 128
STEP = 512
LANES = 128
EPS = 1e-06
F32 = jnp.float32
BF16 = jnp.bfloat16
VMEM_LIMIT = 58 * 1024 * 1024
DOC_SHARE = 4


def dot_nn(left, right):
    return lax.dot_general(left, right, (((1,), (0,)), ((), ())), preferred_element_type=F32)


def dot_nt(left, right):
    return lax.dot_general(left, right, (((1,), (1,)), ((), ())), preferred_element_type=F32)


def dot_tn(left, right):
    return lax.dot_general(left, right, (((0,), (0,)), ((), ())), preferred_element_type=F32)


def head_cols(index, size):
    return slice(index * size, (index + 1) * size)


def scaled_half(array, factor):
    return (array.astype(F32) * factor).astype(BF16)


def spec(shape, index_map):
    return pl.BlockSpec(shape, index_map)


def whole_spec(shape):
    rank = len(shape)
    return pl.BlockSpec(shape, lambda i: (0,) * rank)


def params():
    return pltpu.CompilerParams(vmem_limit_bytes=VMEM_LIMIT)


def cost(flops, bytes_accessed):
    return pl.CostEstimate(flops=flops, bytes_accessed=bytes_accessed, transcendentals=0)


RUN, ENTER, LEAVE, LEAVE_DEV, DOC = range(5)
KEEP, KEEP_TO, KEEP_FROM = range(3)


def count_docs(place, ends):
    total = jnp.zeros_like(place)
    for end in ends:
        total = total + (place >= end).astype(jnp.int32)
    return total


def write_factors(heads, docs, rate_ref, len_ref, first_ref, factor_ref, keep_ref, keep_dev_ref):
    rows = rate_ref.shape[1]
    blocks = rows // BLOCK
    first = first_ref[0]
    ends, total = [], 0
    for i in range(docs):
        total = total + len_ref[i]
        ends.append(total)

    def doc_at(place):
        return jnp.where(place >= 0, count_docs(place, ends), -1)

    upper = (
        lax.broadcasted_iota(jnp.int32, (BLOCK, BLOCK), 0)
        <= lax.broadcasted_iota(jnp.int32, (BLOCK, BLOCK), 1)
    ).astype(F32)
    runs = [
        lax.dot_general(
            rate_ref[:, b * BLOCK : (b + 1) * BLOCK], upper, (((1,), (0,)), ((), ())),
            precision=lax.Precision.HIGHEST, preferred_element_type=F32,
        )
        for b in range(blocks)
    ]
    doc_before = doc_at(first - 1)
    doc_end = doc_at(first + rows - 1)
    filler = jnp.zeros((LANES - DOC * heads - 1, BLOCK), F32)
    keeps = []
    beyond = jnp.zeros((heads, 1), F32)
    for b in reversed(range(blocks)):
        at = slice(b * BLOCK, (b + 1) * BLOCK)
        start = first + b * BLOCK
        doc = count_docs(start + lax.broadcasted_iota(jnp.int32, (1, BLOCK), 1), ends)
        doc_start, doc_last = doc_at(start - 1), doc_at(start + BLOCK - 1)
        run = runs[b]
        last = run[:, BLOCK - 1 : BLOCK]
        factor_ref[RUN * heads : (RUN + 1) * heads, at] = run
        factor_ref[ENTER * heads : (ENTER + 1) * heads, at] = jnp.exp(run) * (doc == doc_start).astype(F32)
        factor_ref[LEAVE * heads : (LEAVE + 1) * heads, at] = jnp.exp(last - run) * (doc == doc_last).astype(F32)
        factor_ref[LEAVE_DEV * heads : (LEAVE_DEV + 1) * heads, at] = (
            jnp.exp(beyond + (last - run)) * (doc == doc_end).astype(F32)
        )
        factor_ref[DOC * heads : DOC * heads + 1, at] = doc.astype(F32)
        factor_ref[DOC * heads + 1 :, at] = filler
        beyond = beyond + last
        keeps.append(jnp.exp(jnp.broadcast_to(last, (heads, LANES))) * (doc_last == doc_start).astype(F32))
    keeps = keeps[::-1]
    to = jnp.ones((heads, LANES), F32)
    for b in range(blocks):
        keep_ref[b, KEEP * heads : (KEEP + 1) * heads, :] = keeps[b]
        keep_ref[b, KEEP_TO * heads : (KEEP_TO + 1) * heads, :] = to
        to = to * keeps[b]
    keep_dev_ref[...] = jnp.exp(jnp.broadcast_to(beyond, (heads, LANES))) * (doc_end == doc_before).astype(F32)
    after = jnp.ones((heads, LANES), F32)
    for b in reversed(range(blocks)):
        keep_ref[b, KEEP_FROM * heads : (KEEP_FROM + 1) * heads, :] = after
        after = after * keeps[b]


def state_kernel(
    heads, size, docs, len_ref, first_ref, rate_ref, key_ref, value_ref,
    state_ref, factor_ref, keep_ref,
):
    step = pl.program_id(0)
    rows = key_ref.shape[0]

    @pl.when(step == 0)
    def _():
        state_ref[...] = jnp.zeros_like(state_ref)
        keep_dev_ref = state_ref.at[heads * size :, :]
        write_factors(heads, docs, rate_ref, len_ref, first_ref, factor_ref, keep_ref, keep_dev_ref)

    at_rows = pl.ds(pl.multiple_of(step * rows, rows), rows)
    for h in range(heads):
        at = head_cols(h, size)
        leave = factor_ref[LEAVE_DEV * heads + h : LEAVE_DEV * heads + h + 1, at_rows]
        state_ref[state_rows(h, size), :] += dot_nn(scaled_half(key_ref[:, at].T, leave), value_ref[:, at])


def local_states(keys, values, rates, lengths, first, heads, size):
    rows, width = keys.shape
    docs = lengths.shape[0]
    step_rows = min(STEP, rows)
    blocks = rows // BLOCK
    shapes = (packed_shape(heads, size), (LANES, rows), (blocks, 3 * heads, LANES))
    smem = pl.BlockSpec(memory_space=pltpu.SMEM)
    return pl.pallas_call(
        functools.partial(state_kernel, heads, size, docs),
        grid=(rows // step_rows,),
        in_specs=[
            smem,
            smem,
            whole_spec((heads, rows)),
            spec((step_rows, width), lambda i: (i, 0)),
            spec((step_rows, width), lambda i: (i, 0)),
        ],
        out_specs=[whole_spec(s) for s in shapes],
        out_shape=[jax.ShapeDtypeStruct(s, F32) for s in shapes],
        compiler_params=params(),
        cost_estimate=cost(2 * rows * width * size, 4 * rows * width),
        name="local_state",
    )(lengths, first, rates, keys, values)


def column(col, group, heads, h):
    return col[:, group * heads + h : group * heads + h + 1]


def block_weights(heads, col, factor_ref, h, bias):
    return jnp.exp(column(col, RUN, heads, h) - factor_ref[RUN * heads + h : RUN * heads + h + 1, :] + bias)


def block_bias(heads, col, factor_ref):
    causal = lax.broadcasted_iota(jnp.int32, (BLOCK, BLOCK), 0) >= lax.broadcasted_iota(
        jnp.int32, (BLOCK, BLOCK), 1
    )
    same = column(col, DOC, heads, 0) == factor_ref[DOC * heads : DOC * heads + 1, :]
    return jnp.where(causal & same, 0.0, -1e30)


def keep_row(keep_ref, group, heads, h):
    return keep_ref[0, group * heads + h : group * heads + h + 1, :]


def forward_kernel(
    heads, size, query_ref, key_ref, value_ref, factor_ref, keep_ref,
    raw_ref, probs_ref, states_ref, query_out_ref, key_out_ref, value_out_ref, state_ref,
):
    step = pl.program_id(0)

    @pl.when(step == 0)
    def _():
        state_ref[...] = jnp.zeros_like(state_ref)

    col = factor_ref[...].T
    bias = block_bias(heads, col, factor_ref)
    for h in range(heads):
        at = head_cols(h, size)
        query, key, value = query_ref[:, at], key_ref[:, at], value_ref[:, at]
        leave = column(col, LEAVE, heads, h)
        keep_from = keep_row(keep_ref, KEEP_FROM, heads, h)
        weights = block_weights(heads, col, factor_ref, h, bias)
        probs = (dot_nt(query, key) * weights).astype(BF16)
        state = state_ref[h]
        state_half = state.astype(BF16)
        probs_ref[0, h] = probs
        states_ref[0, h] = state_half
        entered = query.astype(F32) * column(col, ENTER, heads, h)
        left = key.astype(F32) * leave
        query_out_ref[:, at] = (entered * keep_row(keep_ref, KEEP_TO, heads, h)).astype(BF16)
        key_out_ref[:, at] = (left * keep_from).astype(BF16)
        value_out_ref[:, at] = (value.astype(F32) * leave * keep_from).astype(BF16)
        both = jnp.concatenate([probs, entered.astype(BF16)], axis=1)
        raw = dot_nn(both, jnp.concatenate([value, state_half], axis=0))
        raw_ref[:, at] = raw.astype(BF16)
        state_ref[h] = keep_row(keep_ref, KEEP, heads, h) * state + dot_tn(left.astype(BF16), value)


def forward_local(queries, keys, values, factors, keep, heads, size):
    rows, width = queries.shape
    blocks = rows // BLOCK
    token = spec((BLOCK, width), lambda i: (i, 0))
    per_block = spec((1, heads, size, size), lambda i: (i, 0, 0, 0))
    token_shape = jax.ShapeDtypeStruct((rows, width), BF16)
    return pl.pallas_call(
        functools.partial(forward_kernel, heads, size),
        grid=(blocks,),
        in_specs=[
            token,
            token,
            token,
            spec((LANES, BLOCK), lambda i: (0, i)),
            spec((1,) + keep.shape[1:], lambda i: (i, 0, 0)),
        ],
        out_specs=[token, per_block, per_block, token, token, token],
        out_shape=[
            token_shape,
            jax.ShapeDtypeStruct((blocks, heads, BLOCK, BLOCK), BF16),
            jax.ShapeDtypeStruct((blocks, heads, size, size), BF16),
            token_shape,
            token_shape,
            token_shape,
        ],
        scratch_shapes=[pltpu.VMEM((heads, size, size), F32)],
        compiler_params=params(),
        cost_estimate=cost(8 * rows * width * size, 18 * rows * width),
        name="forward_local",
    )(queries, keys, values, factors, keep)


def state_rows(h, size):
    return slice(h * size, (h + 1) * size)


def entering_state(received, heads, size, h):
    keep_at = slice(heads * size + h, heads * size + h + 1)
    total = received[-1][state_rows(h, size), :]
    for packed in reversed(received[:-1]):
        total = packed[state_rows(h, size), :] + packed[keep_at, :] * total
    return total


def packed_shape(heads, size):
    return (heads * size + heads, LANES)


def raw_kernel(heads, size, hops, raw_ref, query_ref, grad_ref, gain_ref, *rest):
    received = rest[:hops]
    out_ref, sums_ref, enter_ref = rest[hops:]
    step = pl.program_id(0)
    rows = raw_ref.shape[0]

    @pl.when(step == 0)
    def _():
        for h in range(heads):
            enter_ref[h] = entering_state(received, heads, size, h).astype(BF16)

    squares = jnp.zeros((rows, size), F32)
    projected = jnp.zeros((rows, size), F32)
    for h in range(heads):
        at = head_cols(h, size)
        raw = raw_ref[:, at].astype(F32) + dot_nn(query_ref[:, at], enter_ref[h])
        out_ref[:, at] = raw.astype(BF16)
        squares = squares + raw * raw
        projected = projected + grad_ref[:, at].astype(F32) * gain_ref[:, at] * raw
    lane = lax.broadcasted_iota(jnp.int32, (rows, LANES), 1)
    packed = jnp.where(
        lane == 0,
        jnp.sum(squares, axis=1, keepdims=True),
        jnp.where(lane == 1, jnp.sum(projected, axis=1, keepdims=True), 0.0),
    )
    sums_ref[...] = packed.T[0:8, :]


def raw_and_sums(raw, queries, out_grad, gain, received, heads, size):
    rows, width = queries.shape
    step_rows = min(STEP, rows)
    token = spec((step_rows, width), lambda i: (i, 0))
    state_shape = (heads, size, size)
    return pl.pallas_call(
        functools.partial(raw_kernel, heads, size, len(received)),
        grid=(rows // step_rows,),
        in_specs=[
            token,
            token,
            token,
            whole_spec((1, width)),
        ]
        + [whole_spec(packed_shape(heads, size))] * len(received),
        out_specs=[token, spec((8, step_rows), lambda i: (0, i)), whole_spec(state_shape)],
        out_shape=[
            jax.ShapeDtypeStruct((rows, width), BF16),
            jax.ShapeDtypeStruct((8, rows), F32),
            jax.ShapeDtypeStruct(state_shape, BF16),
        ],
        compiler_params=params(),
        cost_estimate=cost(2 * rows * width * size, 8 * rows * width),
        name="raw_and_sums",
    )(raw, queries, out_grad, gain, *received)


def carry_kernel(heads, size, full_width, parts, raw_ref, query_ref, grad_ref, gain_ref, state_in_ref, *rest):
    sums = rest[:parts]
    carry_ref, scale_ref = rest[parts:]
    step = pl.program_id(0)
    rows = raw_ref.shape[0]

    @pl.when(step == 0)
    def _():
        carry_ref[...] = jnp.zeros_like(carry_ref)
        carry_ref[heads * size :, :] = state_in_ref[...]

    total = sums[0][...]
    for part in sums[1:]:
        total = total + part[...]
    total = jnp.concatenate([total, jnp.zeros((LANES - 8, rows), F32)], axis=0).T
    inverse = lax.rsqrt(total[:, 0:1] / full_width + EPS)
    slope = inverse * inverse * inverse * total[:, 1:2] / full_width
    lane = lax.broadcasted_iota(jnp.int32, (rows, LANES), 1)
    scale_ref[...] = jnp.where(lane == 0, inverse, slope)
    for h in range(heads):
        at = head_cols(h, size)
        scaled = grad_ref[:, at].astype(F32) * gain_ref[:, at]
        grad_raw = (inverse * scaled - raw_ref[:, at].astype(F32) * slope).astype(BF16)
        carry_ref[state_rows(h, size), :] += dot_tn(query_ref[:, at], grad_raw)


def carry_states(raw, queries, out_grad, gain, state, sums, full_width, heads, size):
    rows, width = queries.shape
    step_rows = min(STEP, rows)
    token = spec((step_rows, width), lambda i: (i, 0))
    narrow = spec((step_rows, LANES), lambda i: (i, 0))
    packed = packed_shape(heads, size)
    return pl.pallas_call(
        functools.partial(carry_kernel, heads, size, full_width, len(sums)),
        grid=(rows // step_rows,),
        in_specs=[token, token, token, whole_spec((1, width)), spec((heads, LANES), lambda i: (size, 0))]
        + [spec((8, step_rows), lambda i: (0, i))] * len(sums),
        out_specs=[whole_spec(packed), narrow],
        out_shape=[
            jax.ShapeDtypeStruct(packed, F32),
            jax.ShapeDtypeStruct((rows, LANES), F32),
        ],
        compiler_params=params(),
        cost_estimate=cost(2 * rows * width * size, 6 * rows * width),
        name="carry_state",
    )(raw, queries, out_grad, gain, state, *sums)


def backward_kernel(
    heads, size, query_ref, key_ref, value_ref, raw_ref, out_grad_ref, gain_ref, scale_ref,
    factor_ref, keep_ref, probs_ref, states_ref, enter_ref,
    normed_ref, grad_query_ref, grad_key_ref, grad_value_ref, carry_ref,
):
    step = pl.program_id(0)

    @pl.when(step == 0)
    def _():
        carry_ref[...] = jnp.zeros_like(carry_ref)

    col = factor_ref[...].T
    bias = block_bias(heads, col, factor_ref)
    inverse, slope = scale_ref[:, 0:1], scale_ref[:, 1:2]
    for h in range(heads):
        at = head_cols(h, size)
        query, key, value = query_ref[:, at], key_ref[:, at], value_ref[:, at]
        raw, gain = raw_ref[:, at].astype(F32), gain_ref[:, at]
        enter, leave = column(col, ENTER, heads, h), column(col, LEAVE, heads, h)
        grad_raw = (inverse * (out_grad_ref[:, at].astype(F32) * gain) - raw * slope).astype(BF16)
        normed_ref[:, at] = (raw * inverse * gain).astype(BF16)
        weights = block_weights(heads, col, factor_ref, h, bias)
        mixed = (dot_nt(grad_raw, value) * weights).astype(BF16)
        prefix = keep_row(keep_ref, KEEP_TO, heads, h)
        state = (states_ref[0, h].astype(F32) + prefix * enter_ref[h].astype(F32)).astype(BF16)
        grad_query = dot_nn(mixed, key) + enter * dot_nt(grad_raw, state)
        grad_query_ref[:, at] = grad_query.astype(BF16)
        carry = carry_ref[h]
        carry_half = carry.astype(BF16)
        grad_key = dot_tn(mixed, query) + leave * dot_nt(value, carry_half)
        grad_value = dot_tn(probs_ref[0, h], grad_raw) + leave * dot_nn(key, carry_half)
        grad_key_ref[:, at] = grad_key.astype(BF16)
        grad_value_ref[:, at] = grad_value.astype(BF16)
        enter_row = factor_ref[ENTER * heads + h : ENTER * heads + h + 1, :]
        update = dot_nn(scaled_half(query.T, enter_row), grad_raw)
        carry_ref[h] = keep_row(keep_ref, KEEP, heads, h) * carry + update


def backward_local(
    queries, keys, values, raw, out_grad, gain, scale, factors, keep, probs, states, entering, heads, size
):
    rows, width = queries.shape
    blocks = rows // BLOCK
    token = spec((BLOCK, width), lambda i: (blocks - 1 - i, 0))
    narrow = spec((BLOCK, LANES), lambda i: (blocks - 1 - i, 0))
    per_block = spec((1, heads, size, size), lambda i: (blocks - 1 - i, 0, 0, 0))
    return pl.pallas_call(
        functools.partial(backward_kernel, heads, size),
        grid=(blocks,),
        in_specs=[
            token,
            token,
            token,
            token,
            token,
            whole_spec((1, width)),
            narrow,
            spec((LANES, BLOCK), lambda i: (0, blocks - 1 - i)),
            spec((1,) + keep.shape[1:], lambda i: (blocks - 1 - i, 0, 0)),
            per_block,
            per_block,
            whole_spec((heads, size, size)),
        ],
        out_specs=[token] * 4,
        out_shape=[jax.ShapeDtypeStruct((rows, width), BF16)] * 4,
        scratch_shapes=[pltpu.VMEM((heads, size, size), F32)],
        compiler_params=params(),
        cost_estimate=cost(16 * rows * width * size, 22 * rows * width),
        name="backward_local",
    )(queries, keys, values, raw, out_grad, gain, scale, factors, keep, probs, states, entering)


def finish_kernel(heads, size, hops, key_ref, value_ref, grad_key_ref, grad_value_ref, *rest):
    received = rest[:hops]
    key_out_ref, value_out_ref, beyond_ref = rest[hops:]
    step = pl.program_id(0)

    @pl.when(step == 0)
    def _():
        for h in range(heads):
            beyond_ref[h] = entering_state(received, heads, size, h).astype(BF16)

    for h in range(heads):
        at = head_cols(h, size)
        beyond = beyond_ref[h]
        grad_key = grad_key_ref[:, at].astype(F32) + dot_nt(value_ref[:, at], beyond)
        grad_value = grad_value_ref[:, at].astype(F32) + dot_nn(key_ref[:, at], beyond)
        key_out_ref[:, at] = grad_key.astype(BF16)
        value_out_ref[:, at] = grad_value.astype(BF16)


def finish(keys, values, grad_key, grad_value, received, heads, size):
    rows, width = keys.shape
    step_rows = min(STEP, rows)
    token = spec((step_rows, width), lambda i: (i, 0))
    return pl.pallas_call(
        functools.partial(finish_kernel, heads, size, len(received)),
        grid=(rows // step_rows,),
        in_specs=[token] * 4
        + [whole_spec(packed_shape(heads, size))] * len(received),
        out_specs=[token, token],
        out_shape=[jax.ShapeDtypeStruct((rows, width), BF16)] * 2,
        scratch_shapes=[pltpu.VMEM((heads, size, size), BF16)],
        compiler_params=params(),
        cost_estimate=cost(4 * rows * width * size, 12 * rows * width),
        name="finish",
    )(keys, values, grad_key, grad_value, *received)


def from_shards(value, count, away):
    pairs = [(i, i + away) for i in range(count) if 0 <= i + away < count]
    return lax.ppermute(value, "seq", pairs)


def body(queries, keys, values, log_decay, gain, lengths, out_grad):
    rows, heads = log_decay.shape
    width = queries.shape[1]
    size = width // heads
    count = lax.axis_size("seq")
    groups = lax.axis_size("head")
    full_width = width * groups
    longest = rows * count // DOC_SHARE
    hops = max(1, min(count - 1, -(-(longest - 1) // rows)))
    first = (lax.axis_index("seq") * rows).astype(jnp.int32).reshape(1)
    gain = gain.reshape(1, width)

    state, factors, keep = local_states(keys, values, log_decay.T, lengths, first, heads, size)
    before = [from_shards(state, count, j) for j in range(1, hops + 1)]
    raw, probs, states, query_in, key_out, value_out = forward_local(
        queries, keys, values, factors, keep, heads, size
    )
    raw, sums, entering = raw_and_sums(raw, query_in, out_grad, gain, before, heads, size)
    every = [sums] + [
        lax.ppermute(sums, "head", [(i, (i + j) % groups) for i in range(groups)]) for j in range(1, groups)
    ]
    carry, scale = carry_states(raw, query_in, out_grad, gain, state, every, full_width, heads, size)
    after = [from_shards(carry, count, -j) for j in range(1, hops + 1)]
    normed, grad_query, grad_key, grad_value = backward_local(
        queries, keys, values, raw, out_grad, gain, scale, factors, keep, probs, states, entering, heads, size
    )
    grad_key, grad_value = finish(key_out, value_out, grad_key, grad_value, after, heads, size)
    return (normed, grad_query, grad_key, grad_value)


def solution(mesh):
    token = P("seq", "head")
    in_specs = (token, token, token, token, P("head"), P(), token)
    return jax.shard_map(body, mesh=mesh, in_specs=in_specs, out_specs=(token,) * 4, check_vma=False)
```

time: 159 us -> 143 us (0.90)
  the two profiles are of different devices: /device:TPU:10 before, /device:TPU:0 now
where the time goes in v1:
time: 143 us
  Pallas kernels  88.2 us (62%)
  waiting for transfers between devices  37 us (26%)
  starting transfers between devices  14.1 us (10%)
  local copies, waits for them, and re-layouts  2.9 us (2%)
    ppermute x4, waiting for transfers between devices, from_shards(): return lax.ppermute(value, 'seq', pairs)  35 us
    pallas_call x1, Pallas kernels, backward_local(): pl.pallas_call(functools.partial(backward_kernel, heads, size), grid=(blo...  30.4 us
    pallas_call x1, Pallas kernels, forward_local(): pl.pallas_call(functools.partial(forward_kernel, heads, size), grid=(bloc...  24.9 us
    ppermute x4, starting transfers between devices, from_shards(): return lax.ppermute(value, 'seq', pairs)  11.1 us
    pallas_call x1, Pallas kernels, finish(): pl.pallas_call(functools.partial(finish_kernel, heads, size, len(received...  9.85 us
    pallas_call x1, Pallas kernels, carry_states(): pl.pallas_call(functools.partial(carry_kernel, heads, size, full_width, l...  8.6 us
    pallas_call x1, Pallas kernels, raw_and_sums(): pl.pallas_call(functools.partial(raw_kernel, heads, size, len(received)),...  8.43 us
    pallas_call x1, Pallas kernels, local_states(): pl.pallas_call(functools.partial(state_kernel, heads, size, docs), grid=(...  6.09 us
  transfers between devices with their start and end apart: 7, of which 5 were waited for; matrix products, arithmetic and copies ran while one was open for 0% of the time, Pallas kernels for 39%

profile of v1, /device:TPU:0, one launch (start us, length us, event | category | flops | bytes accessed | tf_op | source)
XLA Modules:
  0.0 143.0 jit_solution(16056976337469291861)
XLA Ops:
  0.6 6.1 %local_state.1 = (f32[2064,128]{1,0:T(8,128)}, f32[128,1024]{1,0:T(8,128)}, f32[8,48,128]{2,1,0:T(8,128)}) custom-call(s32[8]{0:T(128)} %len_ref.1, s32[1]{0:T(128)} %bitcast.first_ref, f32[16,1024]{1,0:T(8,128)} %bitcast.6, bf16[1024,2048]{1,0:T(8,128)(2,1)} %key_ref.5, bf16[1024,2048]{1,0:T(8,128)(2,1)} %value_ref.5), custom_call_target="tpu_custom_call" | custom-call | flops 536870912 | bytes 8388608 | tf_op jit(solution)/shard_map/local_state/pallas_call | solution.py:153
  6.7 4.9 %collective-permute-start = (f32[2064,128]{1,0:T(8,128)}, f32[2064,128]{1,0:T(8,128)S(1)}, u32[]{:S(2)}, u32[]{:S(2)}) collective-permute-start(f32[2064,128]{1,0:T(8,128)} %get-tuple-element.28.state_in_ref), channel_id=1, source_target_pairs={{0,4},{4,8},{8,12},{12,16},{16,20},{20,24},{24,28},{1,5},{5,9},{9,... | collective-permute-start | bytes 3170312 | tf_op jit(solution)/shard_map/ppermute | solution.py:487
  11.6 3.5 %collective-permute-start.1 = (f32[2064,128]{1,0:T(8,128)}, f32[2064,128]{1,0:T(8,128)S(1)}, u32[]{:S(2)}, u32[]{:S(2)}) collective-permute-start(f32[2064,128]{1,0:T(8,128)} %get-tuple-element.28.state_in_ref), channel_id=1, source_target_pairs={{0,8},{4,12},{8,16},{12,20},{16,24},{20,28},{1,9},{5,13},{9,17},{1... | collective-permute-start | bytes 3170312 | tf_op jit(solution)/shard_map/ppermute | solution.py:487
  15.1 24.9 %forward_local.1 = (bf16[1024,2048]{1,0:T(8,128)(2,1)}, bf16[8,16,128,128]{3,2,1,0:T(8,128)(2,1)}, bf16[8,16,128,128]{3,2,1,0:T(8,128)(2,1)}, bf16[1024,2048]{1,...) custom-call(bf16[1024,2048]{1,0:T(8,128)(2,1)} %query_ref.3, bf16[1024,2048]{1,0:T(8,128)(2,1)} %key_ref.5, ...), custom_call_target="tpu_custom_call" | custom-call | flops 2147483648 | bytes 37748736 | tf_op jit(solution)/shard_map/forward_local/pallas_call | solution.py:231
  40.0 0.0 collective-permute-done.rest_0_
  40.1 0.0 collective-permute-done.1.rest_1_
  40.1 0.9 copy-done.2
  41.0 0.4 copy-done.3
  41.4 8.4 %raw_and_sums.1 = (bf16[1024,2048]{1,0:T(8,128)(2,1)}, f32[8,1024]{1,0:T(8,128)}, bf16[16,128,128]{2,1,0:T(8,128)(2,1)}) custom-call(bf16[1024,2048]{1,0:T(8,128)(2,1)} %get-tuple-element.26.raw_ref, bf16[1024,2048]{1,0:T(8,128)(2,1)} %get-tuple-element.27.query_ref, bf16[1024,2048]{1,0:T(8,128)(2,1)} %out_grad_ref.1, f32[1,2048]{1,0:T(1,128)} %bitcast.3, ...), custom_call_target="tpu_custom_call" | custom-call | flops 536870912 | bytes 16777216 | tf_op jit(solution)/shard_map/raw_and_sums/pallas_call | solution.py:306
  49.8 0.0 collective-permute-start.2
  49.8 1.6 %collective-permute-start.3 = (f32[8,1024]{1,0:T(8,128)}, f32[8,1024]{1,0:T(8,128)S(1)}, u32[]{:S(2)}, u32[]{:S(2)}) collective-permute-start(f32[8,1024]{1,0:T(8,128)} %get-tuple-element.30.rest_0_), channel_id=1, source_target_pairs={{0,2},{1,3},{2,0},{3,1},{4,6},{5,7},{6,4},{7,5},{8,10},{9,11},{10,... | collective-permute-start | bytes 98312 | tf_op jit(solution)/shard_map/ppermute | solution.py:509
  51.4 1.4 collective-permute-start.4
  52.8 0.6 collective-permute-done.2.rest_1_
  53.4 0.6 collective-permute-done.3.rest_2_
  54.0 0.7 collective-permute-done.4.rest_3_
  54.7 0.6 copy-done.6
  55.3 8.6 %carry_state.1 = (f32[2064,128]{1,0:T(8,128)}, f32[1024,128]{1,0:T(8,128)}) custom-call(bf16[1024,2048]{1,0:T(8,128)(2,1)} %get-tuple-element.29.raw_ref, bf16[1024,2048]{1,0:T(8,128)(2,1)} %get-tuple-element.27.query_ref, bf16[1024,2048]{1,0:T(8,128)(2,1)} %out_grad_ref.1, f32[1,2048]{1,0:T(1,128)} %bitcast.4, f32[2064,128]{1,0:T(8,128)} %get-tuple-element.28.state_in_ref, ...), custom_call_target="tpu_custom_call" | custom-call | flops 536870912 | bytes 12582912 | tf_op jit(solution)/shard_map/carry_state/pallas_call | solution.py:360
  63.9 1.3 collective-permute-start.5
  65.2 1.5 %collective-permute-start.6 = (f32[2064,128]{1,0:T(8,128)}, f32[2064,128]{1,0:T(8,128)S(1)}, u32[]{:S(2)}, u32[]{:S(2)}) collective-permute-start(f32[2064,128]{1,0:T(8,128)} %get-tuple-element.41), channel_id=1, source_target_pairs={{8,0},{12,4},{16,8},{20,12},{24,16},{28,20},{9,1},{13,5},{17,9},{2... | collective-permute-start | bytes 3170312 | tf_op jit(solution)/shard_map/ppermute | solution.py:487
  66.7 30.4 %backward_local.1 = (bf16[1024,2048]{1,0:T(8,128)(2,1)}, bf16[1024,2048]{1,0:T(8,128)(2,1)}, bf16[1024,2048]{1,0:T(8,128)(2,1)}, bf16[1024,2048]{1,0:T(8,128)(2,1)}) custom-call(bf16[1024,2048]{1,0:T(8,128)(2,1)} %query_ref.3, bf16[1024,2048]{1,0:T(8,128)(2,1)} %key_ref.5, bf16[1024,2048]{1,0:T(8,128)(2,1)} %value_ref.5, ...), custom_call_target="tpu_custom_call" | custom-call | flops 4294967296 | bytes 46137344 | tf_op jit(solution)/shard_map/backward_local/pallas_call | solution.py:422
  97.1 11.2 %collective-permute-done.5.rest_0_ = f32[2064,128]{1,0:T(8,128)S(1)} collective-permute-done((f32[2064,128]{1,0:T(8,128)}, f32[2064,128]{1,0:T(8,128)S(1)}, u32[]{:S(2)}, u32[]{:S(2)}) %collective-permute-start.5) | collective-permute-done | bytes 1056800 | tf_op jit(solution)/shard_map/ppermute | solution.py:487
  108.3 23.8 %collective-permute-done.6.rest_1_ = f32[2064,128]{1,0:T(8,128)S(1)} collective-permute-done((f32[2064,128]{1,0:T(8,128)}, f32[2064,128]{1,0:T(8,128)S(1)}, u32[]{:S(2)}, u32[]{:S(2)}) %collective-permute-start.6) | collective-permute-done | bytes 1056800 | tf_op jit(solution)/shard_map/ppermute | solution.py:487
  132.1 1.0 copy-done.1
  133.1 9.8 %finish.1 = (bf16[1024,2048]{1,0:T(8,128)(2,1)}, bf16[1024,2048]{1,0:T(8,128)(2,1)}) custom-call(bf16[1024,2048]{1,0:T(8,128)(2,1)} %get-tuple-element.37.key_ref, bf16[1024,2048]{1,0:T(8,128)(2,1)} %get-tuple-element.38.value_ref, bf16[1024,2048]{1,0:T(8,128)(2,1)} %get-tuple-element.39.grad_key_ref, bf16[1024,2048]{1,0:T(8,128)(2,1)} %get-tuple-element.40.grad_value_ref, ...), custom_call_target="tpu_custom_call" | custom-call | flops 1073741824 | bytes 25165824 | tf_op jit(solution)/shard_map/finish/pallas_call | solution.py:471
  (10 shorter events, 0.0 us)
Async XLA Ops:
  6.7 33.3 %collective-permute-start = (f32[2064,128]{1,0:T(8,128)}, f32[2064,128]{1,0:T(8,128)S(1)}, u32[]{:S(2)}, u32[]{:S(2)}) collective-permute-start(f32[2064,128]{1,0:T(8,128)} %get-tuple-element.28.state_in_ref), channel_id=1, source_target_pairs={{0,4},{4,8},{8,12},{12,16},{16,20},{20,24},{24,28},{1,5},{5,9},{9,... | collective-permute-start | bytes 3170312 | tf_op jit(solution)/shard_map/ppermute | solution.py:487
  11.6 28.4 %collective-permute-start.1 = (f32[2064,128]{1,0:T(8,128)}, f32[2064,128]{1,0:T(8,128)S(1)}, u32[]{:S(2)}, u32[]{:S(2)}) collective-permute-start(f32[2064,128]{1,0:T(8,128)} %get-tuple-element.28.state_in_ref), channel_id=1, source_target_pairs={{0,8},{4,12},{8,16},{12,20},{16,24},{20,28},{1,9},{5,13},{9,17},{1... | collective-permute-start | bytes 3170312 | tf_op jit(solution)/shard_map/ppermute | solution.py:487
  40.1 1.0 copy-start.2
  40.1 1.3 copy-start.3
  49.8 3.6 %collective-permute-start.2 = (f32[8,1024]{1,0:T(8,128)}, f32[8,1024]{1,0:T(8,128)S(1)}, u32[]{:S(2)}, u32[]{:S(2)}) collective-permute-start(f32[8,1024]{1,0:T(8,128)} %get-tuple-element.30.rest_0_), channel_id=1, source_target_pairs={{0,1},{1,2},{2,3},{3,0},{4,5},{5,6},{6,7},{7,4},{8,9},{9,10},{10,1... | collective-permute-start | bytes 98312 | tf_op jit(solution)/shard_map/ppermute | solution.py:509
  49.8 4.2 %collective-permute-start.3 = (f32[8,1024]{1,0:T(8,128)}, f32[8,1024]{1,0:T(8,128)S(1)}, u32[]{:S(2)}, u32[]{:S(2)}) collective-permute-start(f32[8,1024]{1,0:T(8,128)} %get-tuple-element.30.rest_0_), channel_id=1, source_target_pairs={{0,2},{1,3},{2,0},{3,1},{4,6},{5,7},{6,4},{7,5},{8,10},{9,11},{10,... | collective-permute-start | bytes 98312 | tf_op jit(solution)/shard_map/ppermute | solution.py:509
  51.4 3.3 %collective-permute-start.4 = (f32[8,1024]{1,0:T(8,128)}, f32[8,1024]{1,0:T(8,128)S(1)}, u32[]{:S(2)}, u32[]{:S(2)}) collective-permute-start(f32[8,1024]{1,0:T(8,128)} %get-tuple-element.30.rest_0_), channel_id=1, source_target_pairs={{0,3},{1,0},{2,1},{3,2},{4,7},{5,4},{6,5},{7,6},{8,11},{9,8},{10,9... | collective-permute-start | bytes 98312 | tf_op jit(solution)/shard_map/ppermute | solution.py:509
  53.4 1.4 copy-start.4
  54.0 0.7 copy-start.5
  54.7 0.6 copy-start.6
  63.9 44.4 %collective-permute-start.5 = (f32[2064,128]{1,0:T(8,128)}, f32[2064,128]{1,0:T(8,128)S(1)}, u32[]{:S(2)}, u32[]{:S(2)}) collective-permute-start(f32[2064,128]{1,0:T(8,128)} %get-tuple-element.41), channel_id=1, source_target_pairs={{4,0},{8,4},{12,8},{16,12},{20,16},{24,20},{28,24},{5,1},{9,5},{13... | collective-permute-start | bytes 3170312 | tf_op jit(solution)/shard_map/ppermute | solution.py:487
  65.2 66.9 %collective-permute-start.6 = (f32[2064,128]{1,0:T(8,128)}, f32[2064,128]{1,0:T(8,128)S(1)}, u32[]{:S(2)}, u32[]{:S(2)}) collective-permute-start(f32[2064,128]{1,0:T(8,128)} %get-tuple-element.41), channel_id=1, source_target_pairs={{8,0},{12,4},{16,8},{20,12},{24,16},{28,20},{9,1},{13,5},{17,9},{2... | collective-permute-start | bytes 3170312 | tf_op jit(solution)/shard_map/ppermute | solution.py:487
  108.3 23.8 %copy-start = (f32[2064,128]{1,0:T(8,128)}, f32[2064,128]{1,0:T(8,128)S(1)}, u32[]{:S(2)}) copy-start(f32[2064,128]{1,0:T(8,128)S(1)} %collective-permute-done.5.rest_0_) | copy-start | bytes 3170308
  132.1 1.0 copy-start.1
